TPU v7x, 32 devices: a whole 2x2x4 slice. The times are simulated.
32 devices in a mesh: row: 8 (over z, x), reach: 4 (over y, core).
Axes of the slice: x: 2, y: 2, z: 4, core: 2. Of those that a mesh axis runs over, the one named last changes fastest.
Arguments:
- basis: bfloat16 [65536, 128], P(('row', 'reach')), may hold values from -6 to 6
- near_cols: int32 [1024, 7], P(('row', 'reach')), may hold values from 0 to 127, as said below
- near_count: int32 [1024], P(('row', 'reach')), may hold values from 1 to 7
- near_blocks: bfloat16 [1024, 7, 4096], P(('row', 'reach')), may hold values from -0.25 to 0.25
- marker_rows: int32 [512], P(('row', 'reach')), may hold values from 0 to 31
- marker_groups: int32 [512], P(('row', 'reach')), may hold values from 0 to 63, as said below
- marker_count: int32 [32], P(('row', 'reach')), may hold values from 2 to 16
- marker_weights: bfloat16 [512, 4096], P(('row', 'reach')), may hold values from -0.75 to 0.75
- stiffness: float32 [4096], replicated, may hold values from 0.5 to 4
Outputs:
- qfactor: float32 [65536, 128], P(('row', 'reach'))
- rfactor: float32 [128, 128], replicated
Inputs may be any that keep to these rules, and one draw needn't show every extreme that they name: `near_cols`: the first stored block of each block row is the block row itself. `marker_groups`: slot 0 of slab s names group ((64 * s) // 32 + 64 // 2) % 64; slot 1 names (64 * s) // 32; every other slot names that group or the one after it, never beyond 64 - 1.
All inputs are finite; a program needn't handle non-finite values.
Results may differ from a plain program's by a relative error of at most 0.0025.
Values may be sent and summed in bfloat16 or wider, within the bound.
A program may use at most 64 MiB of HBM per device.

v0:
```python
import jax
import jax.numpy as jnp
from jax import lax
from jax.sharding import PartitionSpec as P

BS = 64
NG = 64


def force_of(sums, stiffness):
    scale = lax.rsqrt(1.0 + jnp.mean(sums * sums, axis=1, keepdims=True))
    return (stiffness[:, None] * sums * scale).astype(jnp.bfloat16)


def local(
    basis,
    near_cols,
    near_count,
    near_blocks,
    marker_rows,
    marker_groups,
    marker_count,
    marker_weights,
    stiffness,
):
    slab, stored = near_cols.shape
    width = basis.shape[1]
    side = BS
    slots = marker_rows.shape[0]
    groups = NG
    markers = groups * side
    hp = lax.Precision.HIGHEST
    own = basis.reshape(slab, side, width)
    weights = marker_weights.reshape(slots, side, side)
    mlive = jnp.arange(slots, dtype=jnp.int32) < marker_count[0]
    picked = own[marker_rows]
    partial_value = jnp.einsum("mcj,mcd->mjd", weights, picked, preferred_element_type=jnp.float32)
    partial_flat = partial_value.reshape(slots, side * width)
    onehot = (marker_groups[None, :] == jnp.arange(groups, dtype=jnp.int32)[:, None]) & mlive[
        None, :
    ]
    local_sums = jnp.dot(onehot.astype(jnp.float32), partial_flat, precision=hp).reshape(
        markers, width
    )
    totals = lax.psum(local_sums, ("row", "reach"))
    force = force_of(totals, stiffness)
    force_rows = jnp.dot(
        onehot.T.astype(jnp.bfloat16),
        force.reshape(groups, side * width),
        preferred_element_type=jnp.float32,
    )
    group_basis = lax.all_gather(basis, "reach", axis=0, tiled=True).reshape(-1, side, width)
    live = jnp.arange(stored, dtype=jnp.int32)[None, :] < near_count[:, None]
    fetched = jnp.where(live[:, :, None, None], group_basis[near_cols], jnp.zeros((), jnp.bfloat16))
    blocks = near_blocks.reshape(slab, stored, side, side)
    near = jnp.einsum("bkrc,bkcd->brd", blocks, fetched, preferred_element_type=jnp.float32)
    force_rows = force_rows.astype(jnp.bfloat16).reshape(slots, side, width)
    contrib = jnp.einsum("mcj,mjd->mcd", weights, force_rows, preferred_element_type=jnp.float32)
    rowhot = (
        (marker_rows[None, :] == jnp.arange(slab, dtype=jnp.int32)[:, None]) & mlive[None, :]
    ).astype(jnp.float32)
    spread = jnp.dot(rowhot, contrib.reshape(slots, side * width), precision=hp).reshape(
        slab, side, width
    )
    image = (near + spread).reshape(slab * side, width)
    gram = lax.psum(jnp.dot(image.T, image, precision=hp), ("row", "reach"))
    lower = jnp.linalg.cholesky(gram)
    solved = jax.scipy.linalg.solve_triangular(lower, image.T, lower=True)
    total_rows = slab * side * lax.axis_size(("row", "reach"))
    root = jnp.sqrt(jnp.float32(total_rows))
    return (solved.T * root, lower.T / root)


def solution(mesh):
    return jax.shard_map(
        local,
        mesh=mesh,
        in_specs=(
            P(("row", "reach"), None),
            P(("row", "reach"), None),
            P(("row", "reach")),
            P(("row", "reach"), None, None),
            P(("row", "reach")),
            P(("row", "reach")),
            P(("row", "reach")),
            P(("row", "reach"), None),
            P(),
        ),
        out_specs=(P(("row", "reach"), None), P()),
        check_vma=False,
    )
```

profile of v0, /device:TPU:1, one launch (start us, length us, event | category | flops | bytes accessed | tf_op | source)
XLA Modules:
  0.0 331.3 jit_solution(2423852829834290028)
XLA Ops:
  8.7 0.7 compare_select_fusion.1
  9.4 1.2 reshape.85
  10.5 1.6 gather_fusion.1
  12.2 0.3 fusion.37
  12.5 1.9 fusion.16
  14.3 1.6 reshape.87
  16.0 0.5 all-gather.2.cloned.1.call-update
  16.6 0.1 copy.17
  16.7 0.1 reshape.94
  16.8 0.6 copy-done.1
  17.4 4.9 %reshape.83 = bf16[32,7,64,64]{3,2,0,1:T(8,128)(2,1)} reshape(bf16[32,7,4096]{2,0,1:T(8,128)(2,1)S(1)} %copy-done.1) | data formatting | bytes 3670016 | tf_op jit(solution)/shard_map/reshape | solution.py:55
  22.4 0.1 iota_compare_fusion.3
  22.5 136.2 %all-reduce.3.cloned.1.call-done = f32[4096,128]{1,0:T(8,128)} async-done(((f32[4096,128]{1,0:T(8,128)}), f32[4096,128]{1,0:T(8,128)}) %all-reduce.3.cloned.1.call-update) | async-done | bytes 2097168 | tf_op jit(solution)/shard_map/psum | solution.py:45
  158.7 2.4 multiply_reduce_fusion
  161.1 2.3 multiply_convert_fusion
  163.4 0.7 reshape.88
  164.1 0.3 fusion.15
  164.4 0.1 copy.31
  164.5 0.2 fusion.38
  164.7 0.9 fusion.19
  165.6 4.5 %gather_fusion = bf16[224,64,128]{2,1,0:T(8,128)(2,1)} fusion(bf16[128,64,128]{2,1,0:T(8,128)(2,1)} %bitcast.62, s32[1024]{0:T(1024)S(1)} %pad_clamp_fusion.1), kind=kCustom, calls=%fused_computation | custom fusion | bytes 7340928 | tf_op jit(solution)/shard_map/gather | solution.py:54
  170.1 4.6 %fusion.10 = f32[32,64,128]{2,1,0:T(8,128)S(1)} fusion(bf16[32,7,64,128]{3,2,1,0:T(8,128)(2,1)} %bitcast.63, pred[32,7]{1,0:T(8,128)(4,1)S(1)} %iota_compare_fusion.3, bf16[32,7,64,64]{3,2,0,1:T(8,128)(2,1)} %reshape.83, f32[32,64,128]{2,0,1:T(8,128)S(1)} %fusion.19), kind=kOutput, calls=%fused_computation.12 | convolution fusion | flops 236978176 | bytes 7602400 | tf_op jit(solution)/shard_map/bkrc,bkcd->brd/dot_general | solution.py:56
  174.7 2.4 convolution_bitcast_fusion
  177.2 119.3 %all-reduce.5.cloned.1.call-done = f32[128,128]{0,1:T(8,128)} async-done(((f32[128,128]{0,1:T(8,128)}), f32[128,128]{0,1:T(8,128)}) %all-reduce.5.cloned.1.call-update) | async-done | bytes 65552 | tf_op jit(solution)/shard_map/psum | solution.py:66
  296.6 0.9 copy.23
  297.5 0.9 fusion.23
  298.4 11.7 %cholesky.16 = f32[128,128]{1,0:T(8,128)S(1)} custom-call(f32[128,128]{1,0:T(8,128)S(1)} %fusion.23), custom_call_target="Cholesky" | custom-call | tf_op jit(solution)/shard_map/jit(cholesky)/cholesky | solution.py:67
  310.1 0.6 compare_reduce_fusion
  310.7 0.7 multiply_bitcast_fusion
  311.4 0.7 copy.24
  312.1 9.8 %custom-call.7 = f32[1,128,128]{1,2,0:T(8,128)S(1)} custom-call(f32[1,128,128]{2,1,0:T(8,128)S(1)} %get-tuple-element.7), custom_call_target="InvertDiagBlocksLowerTriangular" | custom-call | tf_op jit(solution)/shard_map/jit(_solve_triangular)/triangular_solve | solution.py:68
  322.0 1.9 convolution_multiply_fusion
  (25 shorter events, 0.3 us)
Async XLA Ops:
  8.0 150.7 %all-reduce.3.cloned.1.call-start = ((), (), s32[]{:S(2)}) async-start(), calls=%async_computation.1 | async-start | bytes 4194304 | tf_op jit(solution)/shard_map/psum | solution.py:45
  15.9 0.7 copy-start.3
  15.9 1.5 copy-start.1
  16.0 149.6 %all-gather.2.cloned.1.call-start = ((), (), s32[]{:S(2)}) async-start(), calls=%async_computation | async-start | bytes 2621440 | tf_op jit(solution)/shard_map/all_gather | solution.py:52
  16.5 280.0 %all-reduce.5.cloned.1.call-start = ((), (), s32[]{:S(2)}) async-start(), calls=%async_computation.2 | async-start | bytes 131072 | tf_op jit(solution)/shard_map/psum | solution.py:66
  17.4 5.0 %copy-start.6 = (s32[32]{0:T(128)S(1)}, s32[32]{0:T(128)}, u32[]{:S(2)}) copy-start(s32[32]{0:T(128)} %param.11) | copy-start | bytes 388
  22.4 138.7 %copy-start.2 = (f32[4096]{0:T(1024)S(1)}, f32[4096]{0:T(1024)}, u32[]{:S(2)}) copy-start(f32[4096]{0:T(1024)} %param.17) | copy-start | bytes 49156
  158.7 2.4 copy-start
  161.1 3.0 copy-start.4
  163.4 1.3 copy-start.5
Sparse Core Ops, SparseCore 0:
  16.1 142.5 all-reduce.2
  177.3 119.1 all-reduce.4
Sparse Core Ops, SparseCore 1:
  18.0 25.5 all-gather.1
where the time goes:
time: 332 us; the launch traced here: 331 us
  waiting for transfers between devices  256 us (77%)
  other arithmetic  29.1 us (9%)
  local copies, waits for them, and re-layouts  17.1 us (5%)
  between operations  16.3 us (5%)
  matrix products  12.5 us (4%)
    psum x1, waiting for transfers between devices, local(): totals = lax.psum(local_sums, ('row', 'reach'))  136 us
    psum x1, waiting for transfers between devices, local(): gram = lax.psum(jnp.dot(image.T, image, precision=hp), ('row', 'reach'))  119 us
    another operation x3, other arithmetic, local(): lower = jnp.linalg.cholesky(gram)  12.4 us
    another operation x1, other arithmetic, local(): solved = jax.scipy.linalg.solve_triangular(lower, image.T, lower=True)  9.81 us
  transfers between devices with their start and end apart: 3, of which 2 were waited for; matrix products, arithmetic and copies ran while one was open for 4% of the time, Pallas kernels for 0%

commit v1 on v0

--- a/solution.py
+++ b/solution.py
@@ -42,7 +42,7 @@
     local_sums = jnp.dot(onehot.astype(jnp.float32), partial_flat, precision=hp).reshape(
         markers, width
     )
-    totals = lax.psum(local_sums, ("row", "reach"))
+    totals = lax.psum(lax.psum(local_sums, "reach"), "row")
     force = force_of(totals, stiffness)
     force_rows = jnp.dot(
         onehot.T.astype(jnp.bfloat16),

time: 332 us -> 364 us (1.096)
  waiting for transfers between devices: 256 us -> 291 us
    all_gather x1, waiting for transfers between devices: 0.03 us -> 17.7 us  [local(): lax.all_gather(basis, 'reach', axis=0, tiled=True).reshape(-1, side, width)]
    psum x1 -> x2, waiting for transfers between devices: 136 us -> 153 us  [local(): totals = lax.psum(lax.psum(local_sums, 'reach'), 'row')]
  transfers between devices with their start and end apart: 3 -> 4, of which waited for: 2 -> 4; matrix products, arithmetic and copies ran while one was open for 4% -> 3% of each run, Pallas kernels for 0% -> 0%
where the time goes in v1:
time: 364 us
  waiting for transfers between devices  291 us (80%)
  other arithmetic  29.1 us (8%)
  local copies, waits for them, and re-layouts  16.4 us (5%)
  between operations  14.6 us (4%)
  matrix products  12.5 us (3%)
    psum x2, waiting for transfers between devices, local(): totals = lax.psum(lax.psum(local_sums, 'reach'), 'row')  153 us
    psum x1, waiting for transfers between devices, local(): gram = lax.psum(jnp.dot(image.T, image, precision=hp), ('row', 'reach'))  119 us
    all_gather x1, waiting for transfers between devices, local(): lax.all_gather(basis, 'reach', axis=0, tiled=True).reshape(-1, side, width)  17.7 us
    another operation x3, other arithmetic, local(): lower = jnp.linalg.cholesky(gram)  12.4 us
    another operation x1, other arithmetic, local(): solved = jax.scipy.linalg.solve_triangular(lower, image.T, lower=True)  9.81 us
  transfers between devices with their start and end apart: 4, of which 4 were waited for; matrix products, arithmetic and copies ran while one was open for 3% of the time, Pallas kernels for 0%

profile of v1, /device:TPU:1, one launch (start us, length us, event | category | flops | bytes accessed | tf_op | source)
XLA Modules:
  0.0 363.5 jit_solution(11165255453511056376)
XLA Ops:
  7.9 0.7 compare_select_fusion.1
  8.5 1.2 reshape.85
  9.7 1.6 gather_fusion.1
  11.4 0.3 fusion.37
  11.6 1.8 fusion.16
  13.4 1.5 reshape.87
  15.0 53.5 %all-reduce.4.cloned.1.call-done = f32[4096,128]{1,0:T(8,128)} async-done(((f32[4096,128]{1,0:T(8,128)}), f32[4096,128]{1,0:T(8,128)}) %all-reduce.4.cloned.1.call-update) | async-done | bytes 2097168 | tf_op jit(solution)/shard_map/psum | solution.py:45
  68.6 0.7 all-gather.2.cloned.1.call-update
  69.4 0.1 copy.17
  69.4 0.1 reshape.94
  69.6 5.0 %reshape.83 = bf16[32,7,64,64]{3,2,0,1:T(8,128)(2,1)} reshape(bf16[32,7,4096]{2,0,1:T(8,128)(2,1)S(1)} %copy-done.1) | data formatting | bytes 3670016 | tf_op jit(solution)/shard_map/reshape | solution.py:55
  74.5 0.1 iota_compare_fusion.3
  74.6 99.8 %all-reduce.6.cloned.1.call-done = f32[4096,128]{1,0:T(8,128)} async-done(((f32[4096,128]{1,0:T(8,128)}), f32[4096,128]{1,0:T(8,128)}) %all-reduce.6.cloned.1.call-update) | async-done | bytes 2097168 | tf_op jit(solution)/shard_map/psum | solution.py:45
  174.4 2.4 multiply_reduce_fusion
  176.8 2.3 multiply_convert_fusion
  179.1 0.7 reshape.88
  179.8 0.3 fusion.15
  180.2 0.2 fusion.38
  180.4 0.9 fusion.19
  181.3 17.7 %all-gather.2.cloned.1.call-done = bf16[8192,128]{1,0:T(8,128)(2,1)} async-done(((bf16[2048,128]{1,0:T(8,128)(2,1)}), bf16[8192,128]{1,0:T(8,128)(2,1)}) %all-gather.2.cloned.1.call-update) | async-done | bytes 2097168 | tf_op jit(solution)/shard_map/all_gather | solution.py:52
  199.0 4.5 %gather_fusion = bf16[224,64,128]{2,1,0:T(8,128)(2,1)} fusion(bf16[128,64,128]{2,1,0:T(8,128)(2,1)} %bitcast.62, s32[1024]{0:T(1024)S(1)} %pad_clamp_fusion.1), kind=kCustom, calls=%fused_computation | custom fusion | bytes 7340928 | tf_op jit(solution)/shard_map/gather | solution.py:54
  203.5 4.6 %fusion.10 = f32[32,64,128]{2,1,0:T(8,128)S(1)} fusion(bf16[32,7,64,128]{3,2,1,0:T(8,128)(2,1)} %bitcast.63, pred[32,7]{1,0:T(8,128)(4,1)S(1)} %iota_compare_fusion.3, bf16[32,7,64,64]{3,2,0,1:T(8,128)(2,1)} %reshape.83, f32[32,64,128]{2,0,1:T(8,128)S(1)} %fusion.19), kind=kOutput, calls=%fused_computation.12 | convolution fusion | flops 236978176 | bytes 7602400 | tf_op jit(solution)/shard_map/bkrc,bkcd->brd/dot_general | solution.py:56
  208.2 2.4 convolution_bitcast_fusion
  210.6 119.0 %all-reduce.8.cloned.1.call-done = f32[128,128]{0,1:T(8,128)} async-done(((f32[128,128]{0,1:T(8,128)}), f32[128,128]{0,1:T(8,128)}) %all-reduce.8.cloned.1.call-update) | async-done | bytes 65552 | tf_op jit(solution)/shard_map/psum | solution.py:66
  329.7 0.9 copy.23
  330.6 0.9 fusion.23
  331.4 11.7 %cholesky.16 = f32[128,128]{1,0:T(8,128)S(1)} custom-call(f32[128,128]{1,0:T(8,128)S(1)} %fusion.23), custom_call_target="Cholesky" | custom-call | tf_op jit(solution)/shard_map/jit(cholesky)/cholesky | solution.py:67
  343.2 0.6 compare_reduce_fusion
  343.8 0.7 multiply_bitcast_fusion
  344.5 0.7 copy.24
  345.2 9.8 %custom-call.7 = f32[1,128,128]{1,2,0:T(8,128)S(1)} custom-call(f32[1,128,128]{2,1,0:T(8,128)S(1)} %get-tuple-element.7), custom_call_target="InvertDiagBlocksLowerTriangular" | custom-call | tf_op jit(solution)/shard_map/jit(_solve_triangular)/triangular_solve | solution.py:68
  355.0 1.9 convolution_multiply_fusion
  (28 shorter events, 0.4 us)
Async XLA Ops:
  7.2 61.4 %all-reduce.4.cloned.1.call-start = ((), (), s32[]{:S(2)}) async-start(), calls=%async_computation.1 | async-start | bytes 4194304 | tf_op jit(solution)/shard_map/psum | solution.py:45
  15.0 54.4 %copy-start.3 = (s32[32,7]{0,1:T(8,128)S(1)}, s32[32,7]{0,1:T(8,128)}, u32[]{:S(2)}) copy-start(s32[32,7]{0,1:T(8,128)} %param.10) | copy-start | bytes 2692
  15.0 54.6 %copy-start.1 = (bf16[32,7,4096]{2,0,1:T(8,128)(2,1)S(1)}, bf16[32,7,4096]{2,0,1:T(8,128)(2,1)}, u32[]{:S(2)}) copy-start(bf16[32,7,4096]{2,0,1:T(8,128)(2,1)} %param.12) | copy-start | bytes 5505028
  15.0 159.4 %all-reduce.6.cloned.1.call-start = ((), (), s32[]{:S(2)}) async-start(), calls=%async_computation.2 | async-start | bytes 4194304 | tf_op jit(solution)/shard_map/psum | solution.py:45
  68.5 130.5 %all-gather.2.cloned.1.call-start = ((), (), s32[]{:S(2)}) async-start(), calls=%async_computation | async-start | bytes 2621440 | tf_op jit(solution)/shard_map/all_gather | solution.py:52
  69.3 260.4 %all-reduce.8.cloned.1.call-start = ((), (), s32[]{:S(2)}) async-start(), calls=%async_computation.3 | async-start | bytes 131072 | tf_op jit(solution)/shard_map/psum | solution.py:66
  69.6 5.0 %copy-start.6 = (s32[32]{0:T(128)S(1)}, s32[32]{0:T(128)}, u32[]{:S(2)}) copy-start(s32[32]{0:T(128)} %param.11) | copy-start | bytes 388
  74.5 102.2 %copy-start.2 = (f32[4096]{0:T(1024)S(1)}, f32[4096]{0:T(1024)}, u32[]{:S(2)}) copy-start(f32[4096]{0:T(1024)} %param.17) | copy-start | bytes 49156
  174.4 2.4 copy-start
  176.8 3.0 copy-start.4
  179.1 1.3 copy-start.5
Sparse Core Ops, SparseCore 0:
  15.1 53.3 all-reduce.3
  72.6 101.7 all-reduce.5
  176.0 22.9 all-gather.1
  210.7 118.8 all-reduce.7
